TPU v7x, 32 devices: a whole 2x2x4 slice. The times are simulated.
32 devices in a mesh: rows: 8 (over z, y), grp: 4 (over x, core).
Axes of the slice: x: 2, y: 2, z: 4, core: 2. Of those that a mesh axis runs over, the one named last changes fastest.
Arguments:
- features: bfloat16 [192, 128, 2048], P('rows', None, 'grp'), may hold values from 0 to 12
- depth_weight: float32 [3, 3, 3, 2048], P(None, None, None, 'grp'), may hold values from -2 to 2
- branch_weight: bfloat16 [4, 2048, 256], P(None, 'grp'), may hold values from -0.125 to 0.125
- pool_weight: bfloat16 [2048, 256], P('grp'), may hold values from -0.125 to 0.125
- proj_weight: bfloat16 [5, 256, 256], P(None, 'grp'), may hold values from -0.15625 to 0.15625
- class_weight: bfloat16 [256, 11], replicated, may hold values from -0.375 to 0.375
- labels: int32 [192, 128], P('rows'), may hold values from 0 to 11
Outputs:
- grad_branch: float32 [4, 2048, 256], P(None, 'grp')
- grad_depth: float32 [3, 3, 3, 2048], P(None, None, None, 'grp')
- grad_pool: float32 [2048, 256], P('grp')
- grad_proj: float32 [5, 256, 256], P(None, 'grp')
- grad_class: float32 [256, 11], replicated
All inputs are finite; a program needn't handle non-finite values.
Results may differ from a plain program's by a relative error of at most 0.0056.
Values may be sent and summed in bfloat16 or wider, within the bound.
A program may use at most 128 MiB of HBM per device.

v0:
```python
import math
import jax
import jax.numpy as jnp
from jax import lax
from jax.sharding import PartitionSpec as P

RATES = (6, 12, 18)
MARGIN = 18


def padded_2(block, sides, width):
    for axis, dim in sides:
        count = lax.axis_size(axis)
        forward = [(i, i + 1) for i in range(count - 1)]
        backward = [(target, source) for source, target in forward]
        low = lax.ppermute(
            lax.slice_in_dim(block, block.shape[dim] - width, None, axis=dim), axis, forward
        )
        high = lax.ppermute(lax.slice_in_dim(block, 0, width, axis=dim), axis, backward)
        block = jnp.concatenate([low, block, high], axis=dim)
    return block


def depth_taps(padded, weights, height, width):
    outputs = []
    for index, rate in enumerate(RATES):
        total = jnp.zeros((height, width, padded.shape[2]), jnp.float32)
        for row_tap in range(3):
            for col_tap in range(3):
                row_start = MARGIN + (row_tap - 1) * rate
                col_start = MARGIN + (col_tap - 1) * rate
                total = (
                    total
                    + weights[index, row_tap, col_tap]
                    * padded[row_start : row_start + height, col_start : col_start + width]
                )
        outputs.append(total.astype(jnp.bfloat16))
    return outputs


def depth_grads(padded, backs, height, width):
    result = []
    for index, rate in enumerate(RATES):
        taps = []
        for row_tap in range(3):
            for col_tap in range(3):
                row_start = MARGIN + (row_tap - 1) * rate
                col_start = MARGIN + (col_tap - 1) * rate
                window = padded[row_start : row_start + height, col_start : col_start + width]
                taps.append(jnp.sum(backs[index] * window, axis=(0, 1)))
        result.append(jnp.stack(taps).reshape(3, 3, -1))
    return jnp.stack(result)


def class_head(mixed, class_weight, labels, total_pixels):
    f32 = jnp.float32
    classes = class_weight.shape[1]
    hidden = jnp.maximum(mixed, 0.0).astype(jnp.bfloat16)
    logits = jnp.einsum("pc,ck->kp", hidden, class_weight, preferred_element_type=f32)
    expo = jnp.exp(logits)
    soft = expo / jnp.sum(expo, axis=0, keepdims=True)
    label_row = labels.reshape(-1)
    onehot = (
        lax.broadcasted_iota(jnp.int32, (classes, label_row.shape[0]), 0) == label_row[None, :]
    ).astype(f32)
    valid = (label_row < classes).astype(f32)
    grad_logit = ((soft - onehot) * valid[None, :] / math.sqrt(total_pixels)).astype(jnp.bfloat16)
    class_part = jnp.einsum("pc,kp->ck", hidden, grad_logit, preferred_element_type=f32)
    back_hidden = jnp.einsum("ck,kp->pc", class_weight, grad_logit, preferred_element_type=f32)
    grad_mixed = (back_hidden * (mixed > 0)).astype(jnp.bfloat16)
    col_total = lax.psum(jnp.sum(grad_mixed.astype(f32), axis=0), "rows")
    return (grad_mixed, col_total, class_part)


def per_device(
    features, depth_weight, branch_weight, pool_weight, proj_weight, class_weight, labels
):
    f32 = jnp.float32
    highest = lax.Precision.HIGHEST
    height, width, local_in = features.shape
    pixels_local = height * width
    total_pixels = height * lax.axis_size("rows") * width
    halo_rows = padded_2(features, (("rows", 0),), MARGIN)
    padded = jnp.pad(halo_rows.astype(f32), ((0, 0), (MARGIN, MARGIN), (0, 0)))
    depth_out = depth_taps(padded, depth_weight, height, width)
    flat_inputs = [item.reshape(pixels_local, local_in) for item in [features] + depth_out]
    column_sum = jnp.sum(features.astype(f32), axis=(0, 1))
    pooled = lax.psum(column_sum, "rows") / total_pixels
    partial_pre = jnp.stack(
        [jnp.dot(flat_inputs[k], branch_weight[k], preferred_element_type=f32) for k in range(4)]
    )
    pool_part = jnp.dot(pooled, pool_weight.astype(f32), precision=highest)[None, None, :]
    pre, pool_pre = (
        lax.psum_scatter(partial_pre, "grp", scatter_dimension=2, tiled=True),
        lax.psum_scatter(pool_part, "grp", scatter_dimension=2, tiled=True),
    )
    pool_pre = pool_pre[0, 0]
    own_out = jnp.maximum(pre, 0.0).astype(jnp.bfloat16)
    own_pool = jnp.maximum(pool_pre, 0.0).astype(jnp.bfloat16)
    mixed_part = jnp.einsum("kpc,kcd->pd", own_out, proj_weight[:4], preferred_element_type=f32)
    mixed_part = (
        mixed_part
        + jnp.dot(own_pool.astype(f32), proj_weight[4].astype(f32), precision=highest)[None, :]
    )
    mixed = lax.psum(mixed_part, "grp")
    grad_mixed, col_total, class_part = class_head(mixed, class_weight, labels, total_pixels)
    back_pre = jnp.einsum("pd,kcd->kpc", grad_mixed, proj_weight[:4], preferred_element_type=f32)
    own_grad = (back_pre * (pre > 0)).astype(jnp.bfloat16)
    own_poolgrad = (
        jnp.dot(col_total, proj_weight[4].astype(f32).T, precision=highest) * (pool_pre > 0)
    ).astype(jnp.bfloat16)
    grad_pre, grad_poolpre = (
        lax.all_gather(own_grad, "grp", axis=2, tiled=True),
        lax.all_gather(own_poolgrad[None, None, :], "grp", axis=2, tiled=True),
    )
    grad_poolpre = grad_poolpre[0, 0]
    proj_part = jnp.einsum("kpc,pd->kcd", own_out, grad_mixed, preferred_element_type=f32)
    pool_proj = own_pool.astype(f32)[:, None] * col_total[None, :]
    branch_part = jnp.stack(
        [
            jnp.einsum("pc,pd->cd", flat_inputs[k], grad_pre[k], preferred_element_type=f32)
            for k in range(4)
        ]
    )
    backs = [
        jnp.einsum(
            "pd,cd->pc", grad_pre[k + 1], branch_weight[k + 1], preferred_element_type=f32
        ).reshape(height, width, local_in)
        for k in range(3)
    ]
    depth_part = depth_grads(padded, backs, height, width)
    grad_pool = pooled[:, None] * grad_poolpre.astype(f32)[None, :]
    grad_branch, grad_depth, proj_main, grad_class = lax.psum(
        (branch_part, depth_part, proj_part, class_part), "rows"
    )
    grad_proj = jnp.concatenate([proj_main, pool_proj[None]], axis=0)
    return (grad_branch, grad_depth, grad_pool, grad_proj, grad_class)


def solution(mesh):
    return jax.shard_map(
        per_device,
        mesh=mesh,
        in_specs=(
            P("rows", None, "grp"),
            P(None, None, None, "grp"),
            P(None, "grp", None),
            P("grp", None),
            P(None, "grp", None),
            P(),
            P("rows", None),
        ),
        out_specs=(
            P(None, "grp", None),
            P(None, None, None, "grp"),
            P("grp", None),
            P(None, "grp", None),
            P(),
        ),
        check_vma=False,
    )
```

profile of v0, /device:TPU:0, one launch (start us, length us, event | category | flops | bytes accessed | tf_op | source)
XLA Modules:
  0.0 927.9 jit_solution(12588569372178841400)
XLA Ops:
  7.2 5.2 fusion.69
  12.4 6.3 collective-permute-start
  18.7 1.3 collective-permute-start.1
  20.4 110.5 %psum.49 = f32[512]{0:T(512)S(1)} all-reduce(f32[512]{0:T(512)S(1)} %convert_reduce_fusion), channel_id=1, replica_groups=mesh['rows'=8,'grp'=4] {'rows'}, use_global_device_ids=true, to_apply=%region_2.3 | all-reduce | flops 512 | bytes 4096 | tf_op jit(solution)/shard_map/psum | solution.py:88
  132.2 1.9 convolution_bitcast_fusion.5
  134.2 8.1 maximum_convert_fusion
  142.3 24.1 %add_convert_fusion.1 = bf16[24,128,512]{2,1,0:T(8,128)(2,1)S(1)} fusion(f32[60,128,512]{2,1,0:T(8,128)} %maximum_convert_fusion, f32[512]{0:T(512)S(1)} %bitcast.242, f32[512]{0:T(512)S(1)} %bitcast.243, f32[512]{0:T(512)S(1)} %bitcast.244, f32[512]{0:T(512)S(1)} %bitcast.245, f32[512]{0:T(512)S(1)} %bitcast.246, f32[512]{0:T(512)S(1)} %bitcast.247, ...), kind=kLoop, calls=%fused_computation.49 | loop fusion | flops 28311552 | bytes 37767168 | tf_op jit(solution)/shard_map/convert_element_type | solution.py:37
  166.3 2.1 convolution_bitcast_fusion.3
  168.5 19.2 %add_convert_fusion = bf16[24,128,512]{2,1,0:T(8,128)(2,1)S(1)} fusion(f32[60,128,512]{2,1,0:T(8,128)} %maximum_convert_fusion, f32[512]{0:T(512)S(1)} %bitcast.230, f32[512]{0:T(512)S(1)} %bitcast.231, f32[512]{0:T(512)S(1)} %bitcast.235, f32[512]{0:T(512)S(1)} %bitcast.236, f32[512]{0:T(512)S(1)} %bitcast.237, f32[512]{0:T(512)S(1)} %bitcast.238, ...), kind=kLoop, calls=%fused_computation.48 | loop fusion | flops 28311552 | bytes 37767168 | tf_op jit(solution)/shard_map/convert_element_type | solution.py:37
  187.7 1.7 copy-done.3
  189.4 3.6 convolution_bitcast_fusion.2
  193.0 24.6 %add_convert_fusion.2 = bf16[24,128,512]{2,1,0:T(8,128)(2,1)S(1)} fusion(f32[60,128,512]{2,1,0:T(8,128)} %maximum_convert_fusion, f32[512]{0:T(512)S(1)} %bitcast.233, f32[512]{0:T(512)S(1)} %bitcast.234, f32[512]{0:T(512)S(1)} %bitcast.225, f32[512]{0:T(512)S(1)} %bitcast.226, f32[512]{0:T(512)S(1)} %bitcast.227, f32[512]{0:T(512)S(1)} %bitcast.228, ...), kind=kLoop, calls=%fused_computation.50 | loop fusion | flops 28311552 | bytes 37767168 | tf_op jit(solution)/shard_map/convert_element_type | solution.py:37
  217.6 1.6 copy-done.5
  219.2 2.4 convolution_bitcast_fusion.4
  221.6 4.9 pad_maximum_fusion
  226.5 15.3 %copy.30 = f32[4,3072,256]{1,0,2:T(4,128)} copy(f32[4,3072,256]{2,1,0:T(8,128)} %pad_maximum_fusion) | data formatting | bytes 25165824 | tf_op jit(solution)/shard_map/stack | solution.py:89
  244.8 217.1 %all-reduce.12.cloned.1.call-done = f32[4,3072,256]{1,0,2:T(4,128)} async-done(((f32[4,3072,256]{1,0,2:T(4,128)}), f32[4,3072,256]{1,0,2:T(4,128)}) %all-reduce.12.cloned.1.call-update) | async-done | bytes 12582928
  461.9 2.1 constant_dynamic-slice_fusion
  464.0 1.6 copy-done.7
  465.6 3.8 fusion.1
  469.5 68.7 %all-reduce.10.cloned.1.call-done = f32[3072,256]{1,0:T(8,128)} async-done(((f32[3072,256]{1,0:T(8,128)}), f32[3072,256]{1,0:T(8,128)}) %all-reduce.10.cloned.1.call-update) | async-done | bytes 3145744 | tf_op jit(solution)/shard_map/psum | solution.py:105
  538.2 2.6 fusion.73
  540.8 3.2 convert_reduce_fusion.1
  544.1 3.3 fusion.3
  547.4 2.4 copy.33
  549.8 2.8 fusion.29
  552.7 5.0 fusion.12
  557.7 38.8 %all-gather.3.cloned.1.call-done = bf16[4,3072,256]{1,0,2:T(4,128)(2,1)} async-done(((bf16[4,3072,64]{1,0,2:T(4,128)(2,1)}), bf16[4,3072,256]{1,0,2:T(4,128)(2,1)}) %all-gather.3.cloned.1.call-update) | async-done | bytes 6291472 | tf_op jit(solution)/shard_map/all_gather | solution.py:113
  596.4 18.7 %fusion.68 = (bf16[1,3072,256]{1,0,2:T(2,128)(2,1)}, bf16[1,3072,256]{1,0,2:T(2,128)(2,1)}, bf16[1,3072,256]{1,0,2:T(2,128)(2,1)}, bf16[1,3072,256]{1,0,2:T(2,128)(2,1)}) fusion(bf16[4,3072,256]{1,0,2:T(4,128)(2,1)} %all-gather.3.cloned.1.call-done), kind=kLoop, calls=%fused_computation.133 | loop fusion | bytes 12582912 | tf_op jit(solution)/shard_map/slice | solution.py:121
  615.2 7.3 copy.48
  622.5 4.3 fusion.18
  626.8 24.8 %multiply_reduce_fusion.18 = (f32[512]{0:T(512)S(1)}, f32[512]{0:T(512)S(1)}, f32[512]{0:T(512)S(1)}, f32[512]{0:T(512)S(1)}, f32[512]{0:T(512)S(1)}, /*index=5*...) fusion(f32[60,128,512]{2,1,0:T(8,128)} %maximum_convert_fusion, ...), kind=kOutput, calls=%fused_computation.38 | convolution fusion | flops 833613312 | bytes 36456448 | tf_op jit(solution)/shard_map/pd,cd->pc/dot_general | solution.py:126
  651.6 7.3 copy.49
  658.9 4.3 fusion.21
  663.2 24.1 %multiply_reduce_fusion.9 = (f32[512]{0:T(512)S(1)}, f32[512]{0:T(512)S(1)}, f32[512]{0:T(512)S(1)}, f32[512]{0:T(512)S(1)}, f32[512]{0:T(512)S(1)}, /*index=5*/...) fusion(f32[60,128,512]{2,1,0:T(8,128)} %maximum_convert_fusion, ...), kind=kOutput, calls=%fused_computation.29 | convolution fusion | flops 833613312 | bytes 36456448 | tf_op jit(solution)/shard_map/pd,cd->pc/dot_general | solution.py:126
  687.4 7.3 copy.50
  694.7 4.2 fusion.24
  698.9 20.2 %multiply_reduce_fusion = (f32[512]{0:T(512)S(1)}, f32[512]{0:T(512)S(1)}, f32[512]{0:T(512)S(1)}, f32[512]{0:T(512)S(1)}, f32[512]{0:T(512)S(1)}, /*index=5*/f3...) fusion(f32[60,128,512]{2,1,0:T(8,128)} %maximum_convert_fusion, bf16[24,128,256]{2,1,0:T(8,128)(2,1)} %bitcast.217, ...), kind=kOutput, calls=%fused_computation.20 | convolution fusion | flops 833613312 | bytes 36456448 | tf_op jit(solution)/shard_map/pd,cd->pc/dot_general | solution.py:126
  719.2 7.3 copy.47
  726.5 3.2 fusion.15
  730.5 3.0 pad_maximum_fusion.1
  734.1 66.5 %all-reduce.14.cloned.1.call-done = (f32[3,3,3,512]{3,2,1,0:T(4,128)}, f32[256]{0:T(256)}, f32[256,11]{0,1:T(8,128)}) async-done(((f32[3,3,3,512]{3,2,1,0:T(4,128)}, f32[256]{0:T(256)}, f32[256,11]{0,1:T(8,128)}), (f32[3,3,3,512]{3,2,1,0:T(4,128)}, f32[256]{0:T(256)}, f32[256,11]{0,1:T(8,128)})) %all-reduce.14.cloned.1.call-update) | async-done | bytes 67600 | tf_op jit(solution)/shard_map/psum | solution.py:133
  801.8 5.6 all-reduce.1
  809.1 104.3 %all-reduce.16.cloned.1.call-done = (f32[4,512,256]{1,2,0:T(8,128)}, f32[4,64,256]{2,1,0:T(8,128)}) async-done(((f32[4,512,256]{1,2,0:T(8,128)}, f32[4,64,256]{2,1,0:T(8,128)}), (f32[4,512,256]{1,2,0:T(8,128)}, f32[4,64,256]{2,1,0:T(8,128)})) %all-reduce.16.cloned.1.call-update) | async-done | bytes 2359312 | tf_op jit(solution)/shard_map/psum | solution.py:133
  913.4 2.9 copy.41
  916.3 1.7 pad_maximum_fusion.2
  918.0 1.5 copy.63
  919.5 1.3 copy.64
  (69 shorter events, 7.9 us)
Async XLA Ops:
  7.2 123.8 %copy-start = (bf16[512,256]{1,0:T(8,128)(2,1)S(1)}, bf16[512,256]{1,0:T(8,128)(2,1)}, u32[]{:S(2)}) copy-start(bf16[512,256]{1,0:T(8,128)(2,1)} %param.10) | copy-start | bytes 786436
  7.2 12.8 %copy-start.2 = (bf16[24,128,512]{2,1,0:T(8,128)(2,1)S(1)}, bf16[24,128,512]{2,1,0:T(8,128)(2,1)}, u32[]{:S(2)}) copy-start(bf16[24,128,512]{2,1,0:T(8,128)(2,1)} %param.7) | copy-start | bytes 9437188
  7.2 125.0 %copy-start.13 = (f32[3,3,3,512]{3,2,1,0:T(4,128)S(1)}, f32[3,3,3,512]{3,2,1,0:T(4,128)}, u32[]{:S(2)}) copy-start(f32[3,3,3,512]{3,2,1,0:T(4,128)} %param.8) | copy-start | bytes 165892
  7.2 236.6 %reduce-scatter.4.cloned.1.call-start = ((), (), s32[]{:S(2)}) async-start(), calls=%async_computation.3 | async-start | bytes 163840
  12.4 121.8 %collective-permute-start = (bf16[18,128,512]{2,1,0:T(8,128)(2,1)}, bf16[18,128,512]{2,1,0:T(8,128)(2,1)}, u32[]{:S(2)}, u32[]{:S(2)}) collective-permute-start(bf16[18,128,512]{2,1,0:T(8,128)(2,1)} %get-tuple-element.56), channel_id=1, source_target_pairs={{0,4},{4,8},{8,12},{12,16},{16,20},{20,24},{24,28},{1,5},{5,9},{9,... | collective-permute-start | bytes 7077896 | tf_op jit(solution)/shard_map/ppermute | solution.py:16
  18.7 115.5 %collective-permute-start.1 = (bf16[18,128,512]{2,1,0:T(8,128)(2,1)}, bf16[18,128,512]{2,1,0:T(8,128)(2,1)}, u32[]{:S(2)}, u32[]{:S(2)}) collective-permute-start(bf16[18,128,512]{2,1,0:T(8,128)(2,1)} %get-tuple-element.57), channel_id=1, source_target_pairs={{4,0},{8,4},{12,8},{16,12},{20,16},{24,20},{28,24},{5,1},{9,5},{13... | collective-permute-start | bytes 7077896 | tf_op jit(solution)/shard_map/ppermute | solution.py:19
  132.1 329.7 %all-reduce.12.cloned.1.call-start = ((), (), s32[]{:S(2)}) async-start(), calls=%async_computation.4 | async-start | bytes 25165824
  166.3 2.1 copy-start.4
  187.7 1.7 copy-start.3
  217.6 1.6 copy-start.5
  217.6 4.0 copy-start.6
  241.8 0.7 copy-start.16
  241.8 2.8 copy-start.15
  241.9 296.4 %all-reduce.10.cloned.1.call-start = ((), (), s32[]{:S(2)}) async-start(), calls=%async_computation.1 | async-start | bytes 6291456 | tf_op jit(solution)/shard_map/psum | solution.py:105
  464.0 1.7 copy-start.7
  464.0 5.5 copy-start.12
  464.0 74.3 %copy-start.14 = (bf16[256,11]{0,1:T(8,128)(2,1)S(1)}, bf16[256,11]{0,1:T(8,128)(2,1)}, u32[]{:S(2)}) copy-start(bf16[256,11]{0,1:T(8,128)(2,1)} %param.12) | copy-start | bytes 16900
  469.4 127.0 %all-gather.3.cloned.1.call-start = ((), (), s32[]{:S(2)}) async-start(), calls=%async_computation.2 | async-start | bytes 7864320 | tf_op jit(solution)/shard_map/all_gather | solution.py:113
  538.2 5.8 copy-start.8
  544.1 3.3 copy-start.9
  549.8 250.9 %all-reduce.14.cloned.1.call-start = ((), (), s32[]{:S(2)}) async-start(), calls=%async_computation.5 | async-start | bytes 182272 | tf_op jit(solution)/shard_map/psum | solution.py:133
  622.5 4.3 copy-start.10
  658.9 4.3 copy-start.11
  726.5 194.3 %copy-start.1 = (bf16[512,256]{1,0:T(8,128)(2,1)S(1)}, bf16[512,256]{1,0:T(8,128)(2,1)}, u32[]{:S(2)}) copy-start(bf16[512,256]{1,0:T(8,128)(2,1)} %param.10) | copy-start | bytes 786436
  730.4 183.0 %all-reduce.16.cloned.1.call-start = ((), (), s32[]{:S(2)}) async-start(), calls=%async_computation.6 | async-start | bytes 4718592 | tf_op jit(solution)/shard_map/psum | solution.py:133
Sparse Core Ops, SparseCore 0:
  132.2 18.7 reduce-scatter.3
  242.0 219.8 all-reduce.11
  469.5 68.6 all-reduce.9
  549.9 46.4 all-gather.2
  730.5 70.0 all-reduce.13
  805.1 108.2 all-reduce.15
where the time goes:
time: 932 us; the launch traced here: 928 us
  waiting for transfers between devices  496 us (53%)
  matrix products  118 us (13%)
  blocking collectives  116 us (12%)
  other arithmetic  88.4 us (9%)
  local copies, waits for them, and re-layouts  85.7 us (9%)
  between operations  15.9 us (2%)
    unnamed x8, waiting for transfers between devices  217 us
    psum x2, waiting for transfers between devices, per_device(): lax.psum((branch_part, depth_part, proj_part, class_part), 'rows')  171 us
    psum x1, blocking collectives, per_device(): pooled = lax.psum(column_sum, 'rows') / total_pixels  111 us
    dot_general x3, matrix products, per_device(): jnp.einsum('pd,cd->pc', grad_pre[k + 1], branch_weight[k + 1], preferred_...  69 us
    psum x1, waiting for transfers between devices, per_device(): mixed = lax.psum(mixed_part, 'grp')  68.7 us
    convert_element_type x3, other arithmetic, depth_taps(): outputs.append(total.astype(jnp.bfloat16))  67.9 us
    unnamed x46, local copies, waits for them, and re-layouts  43.9 us
    all_gather x1, waiting for transfers between devices, per_device(): lax.all_gather(own_grad, 'grp', axis=2, tiled=True)  38.8 us
  transfers between devices with their start and end apart: 8, of which 5 were waited for; matrix products, arithmetic and copies ran while one was open for 13% of the time, Pallas kernels for 0%

commit v1 on v0

--- a/solution.py
+++ b/solution.py
@@ -6,6 +6,14 @@
 
 RATES = (6, 12, 18)
 MARGIN = 18
+
+
+def doubling_sum(shard, mesh_axis):
+    n_dev, total = (lax.axis_size(mesh_axis), shard)
+    for far in [1 << k for k in range(n_dev.bit_length() - 1)]:
+        pairs = [(i, i ^ far) for i in range(n_dev)]
+        total = total + lax.ppermute(total, mesh_axis, pairs)
+    return total
 
 
 def padded_2(block, sides, width):
@@ -102,7 +110,7 @@
         mixed_part
         + jnp.dot(own_pool.astype(f32), proj_weight[4].astype(f32), precision=highest)[None, :]
     )
-    mixed = lax.psum(mixed_part, "grp")
+    mixed = doubling_sum(mixed_part, "grp")
     grad_mixed, col_total, class_part = class_head(mixed, class_weight, labels, total_pixels)
     back_pre = jnp.einsum("pd,kcd->kpc", grad_mixed, proj_weight[:4], preferred_element_type=f32)
     own_grad = (back_pre * (pre > 0)).astype(jnp.bfloat16)

time: 932 us -> 932 us (level)
    ppermute x0 -> x2, waiting for transfers between devices: none -> 75.2 us  [doubling_sum(): total = total + lax.ppermute(total, mesh_axis, pairs)]
    psum x1 -> x0, waiting for transfers between devices: 68.7 us -> none  [per_device(): mixed = lax.psum(mixed_part, 'grp')]
    unnamed x46 -> x48, local copies, waits for them, and re-layouts: 43.9 us -> 42.3 us
    unnamed x8 -> x7, waiting for transfers between devices: 217 us -> 217 us
  transfers between devices with their start and end apart: 8 -> 9, of which waited for: 5 -> 6; matrix products, arithmetic and copies ran while one was open for 13% -> 13% of each run, Pallas kernels for 0% -> 0%
where the time goes in v1:
time: 932 us; the launch traced here: 928 us
  waiting for transfers between devices  503 us (54%)
  blocking collectives  116 us (12%)
  matrix products  111 us (12%)
  other arithmetic  89.3 us (10%)
  local copies, waits for them, and re-layouts  84.1 us (9%)
  between operations  15.6 us (2%)
    unnamed x7, waiting for transfers between devices  217 us
    psum x2, waiting for transfers between devices, per_device(): lax.psum((branch_part, depth_part, proj_part, class_part), 'rows')  171 us
    psum x1, blocking collectives, per_device(): pooled = lax.psum(column_sum, 'rows') / total_pixels  111 us
    ppermute x2, waiting for transfers between devices, doubling_sum(): total = total + lax.ppermute(total, mesh_axis, pairs)  75.2 us
    dot_general x3, matrix products, per_device(): jnp.einsum('pd,cd->pc', grad_pre[k + 1], branch_weight[k + 1], preferred_...  69 us
    convert_element_type x3, other arithmetic, depth_taps(): outputs.append(total.astype(jnp.bfloat16))  67.9 us
    unnamed x48, local copies, waits for them, and re-layouts  42.3 us
    all_gather x1, waiting for transfers between devices, per_device(): lax.all_gather(own_grad, 'grp', axis=2, tiled=True)  39.3 us
  transfers between devices with their start and end apart: 9, of which 6 were waited for; matrix products, arithmetic and copies ran while one was open for 13% of the time, Pallas kernels for 0%

profile of v1, /device:TPU:0, one launch (start us, length us, event | category | flops | bytes accessed | tf_op | source)
XLA Modules:
  0.0 927.5 jit_solution(9652420252882506472)
XLA Ops:
  7.2 5.2 fusion.69
  12.4 6.3 collective-permute-start
  18.7 1.3 collective-permute-start.1
  20.4 110.5 %psum.42 = f32[512]{0:T(512)S(1)} all-reduce(f32[512]{0:T(512)S(1)} %convert_reduce_fusion), channel_id=1, replica_groups=mesh['rows'=8,'grp'=4] {'rows'}, use_global_device_ids=true, to_apply=%region_2.3 | all-reduce | flops 512 | bytes 4096 | tf_op jit(solution)/shard_map/psum | solution.py:96
  131.0 1.1 convolution_bitcast_fusion.6
  132.2 1.9 convolution_bitcast_fusion.5
  134.2 8.1 maximum_convert_fusion
  142.3 24.1 %add_convert_fusion.1 = bf16[24,128,512]{2,1,0:T(8,128)(2,1)S(1)} fusion(f32[60,128,512]{2,1,0:T(8,128)} %maximum_convert_fusion, f32[512]{0:T(512)S(1)} %bitcast.246, f32[512]{0:T(512)S(1)} %bitcast.247, f32[512]{0:T(512)S(1)} %bitcast.248, f32[512]{0:T(512)S(1)} %bitcast.249, f32[512]{0:T(512)S(1)} %bitcast.250, f32[512]{0:T(512)S(1)} %bitcast.251, ...), kind=kLoop, calls=%fused_computation.49 | loop fusion | flops 28311552 | bytes 37767168 | tf_op jit(solution)/shard_map/convert_element_type | solution.py:45
  166.3 2.1 convolution_bitcast_fusion.3
  168.5 19.2 %add_convert_fusion = bf16[24,128,512]{2,1,0:T(8,128)(2,1)S(1)} fusion(f32[60,128,512]{2,1,0:T(8,128)} %maximum_convert_fusion, f32[512]{0:T(512)S(1)} %bitcast.234, f32[512]{0:T(512)S(1)} %bitcast.235, f32[512]{0:T(512)S(1)} %bitcast.239, f32[512]{0:T(512)S(1)} %bitcast.240, f32[512]{0:T(512)S(1)} %bitcast.241, f32[512]{0:T(512)S(1)} %bitcast.242, ...), kind=kLoop, calls=%fused_computation.48 | loop fusion | flops 28311552 | bytes 37767168 | tf_op jit(solution)/shard_map/convert_element_type | solution.py:45
  187.7 1.7 copy-done.3
  189.4 3.6 convolution_bitcast_fusion.2
  193.0 24.6 %add_convert_fusion.2 = bf16[24,128,512]{2,1,0:T(8,128)(2,1)S(1)} fusion(f32[60,128,512]{2,1,0:T(8,128)} %maximum_convert_fusion, f32[512]{0:T(512)S(1)} %bitcast.237, f32[512]{0:T(512)S(1)} %bitcast.238, f32[512]{0:T(512)S(1)} %bitcast.229, f32[512]{0:T(512)S(1)} %bitcast.230, f32[512]{0:T(512)S(1)} %bitcast.231, f32[512]{0:T(512)S(1)} %bitcast.232, ...), kind=kLoop, calls=%fused_computation.50 | loop fusion | flops 28311552 | bytes 37767168 | tf_op jit(solution)/shard_map/convert_element_type | solution.py:45
  217.6 1.6 copy-done.5
  219.2 2.4 convolution_bitcast_fusion.4
  221.6 4.9 pad_maximum_fusion
  226.5 15.3 %copy.30 = f32[4,3072,256]{1,0,2:T(4,128)} copy(f32[4,3072,256]{2,1,0:T(8,128)} %pad_maximum_fusion) | data formatting | bytes 25165824 | tf_op jit(solution)/shard_map/stack | solution.py:97
  244.8 217.1 %all-reduce.9.cloned.1.call-done = f32[4,3072,256]{1,0,2:T(4,128)} async-done(((f32[4,3072,256]{1,0,2:T(4,128)}), f32[4,3072,256]{1,0,2:T(4,128)}) %all-reduce.9.cloned.1.call-update) | async-done | bytes 12582928
  461.9 2.1 constant_dynamic-slice_fusion
  464.0 2.1 fusion.1
  466.2 5.6 collective-permute-done.2
  472.9 69.6 %collective-permute-done.3 = f32[3072,256]{1,0:T(8,128)S(1)} collective-permute-done((f32[3072,256]{1,0:T(8,128)S(1)}, f32[3072,256]{1,0:T(8,128)S(1)}, u32[]{:S(2)}, u32[]{:S(2)}) %collective-permute-start.3) | collective-permute-done | bytes 3145760 | tf_op jit(solution)/shard_map/ppermute | solution.py:15
  543.6 1.4 convert_reduce_fusion.1
  544.9 2.3 fusion.2
  547.3 2.4 copy.33
  549.7 2.3 fusion.62
  552.0 5.0 fusion.11
  557.1 39.3 %all-gather.3.cloned.1.call-done = bf16[4,3072,256]{1,0,2:T(4,128)(2,1)} async-done(((bf16[4,3072,64]{1,0,2:T(4,128)(2,1)}), bf16[4,3072,256]{1,0,2:T(4,128)(2,1)}) %all-gather.3.cloned.1.call-update) | async-done | bytes 6291472 | tf_op jit(solution)/shard_map/all_gather | solution.py:121
  596.4 18.7 %fusion.68 = (bf16[1,3072,256]{1,0,2:T(2,128)(2,1)}, bf16[1,3072,256]{1,0,2:T(2,128)(2,1)}, bf16[1,3072,256]{1,0,2:T(2,128)(2,1)}, bf16[1,3072,256]{1,0,2:T(2,128)(2,1)}) fusion(bf16[4,3072,256]{1,0,2:T(4,128)(2,1)} %all-gather.3.cloned.1.call-done), kind=kLoop, calls=%fused_computation.131 | loop fusion | bytes 12582912 | tf_op jit(solution)/shard_map/slice | solution.py:129
  615.1 7.3 copy.48
  622.5 4.3 fusion.17
  626.8 24.8 %multiply_reduce_fusion.18 = (f32[512]{0:T(512)S(1)}, f32[512]{0:T(512)S(1)}, f32[512]{0:T(512)S(1)}, f32[512]{0:T(512)S(1)}, f32[512]{0:T(512)S(1)}, /*index=5*...) fusion(f32[60,128,512]{2,1,0:T(8,128)} %maximum_convert_fusion, ...), kind=kOutput, calls=%fused_computation.38 | convolution fusion | flops 833613312 | bytes 36456448 | tf_op jit(solution)/shard_map/pd,cd->pc/dot_general | solution.py:134
  651.6 7.3 copy.49
  658.9 4.3 fusion.20
  663.2 24.1 %multiply_reduce_fusion.9 = (f32[512]{0:T(512)S(1)}, f32[512]{0:T(512)S(1)}, f32[512]{0:T(512)S(1)}, f32[512]{0:T(512)S(1)}, f32[512]{0:T(512)S(1)}, /*index=5*/...) fusion(f32[60,128,512]{2,1,0:T(8,128)} %maximum_convert_fusion, ...), kind=kOutput, calls=%fused_computation.29 | convolution fusion | flops 833613312 | bytes 36456448 | tf_op jit(solution)/shard_map/pd,cd->pc/dot_general | solution.py:134
  687.4 7.3 copy.50
  694.7 4.2 fusion.23
  698.9 20.2 %multiply_reduce_fusion = (f32[512]{0:T(512)S(1)}, f32[512]{0:T(512)S(1)}, f32[512]{0:T(512)S(1)}, f32[512]{0:T(512)S(1)}, f32[512]{0:T(512)S(1)}, /*index=5*/f3...) fusion(f32[60,128,512]{2,1,0:T(8,128)} %maximum_convert_fusion, bf16[24,128,256]{2,1,0:T(8,128)(2,1)} %bitcast.221, ...), kind=kOutput, calls=%fused_computation.20 | convolution fusion | flops 833613312 | bytes 36456448 | tf_op jit(solution)/shard_map/pd,cd->pc/dot_general | solution.py:134
  719.1 7.3 copy.47
  726.5 3.2 fusion.14
  730.4 3.0 pad_maximum_fusion.1
  734.1 66.5 %all-reduce.11.cloned.1.call-done = (f32[3,3,3,512]{3,2,1,0:T(4,128)}, f32[256]{0:T(256)}, f32[256,11]{0,1:T(8,128)}) async-done(((f32[3,3,3,512]{3,2,1,0:T(4,128)}, f32[256]{0:T(256)}, f32[256,11]{0,1:T(8,128)}), (f32[3,3,3,512]{3,2,1,0:T(4,128)}, f32[256]{0:T(256)}, f32[256,11]{0,1:T(8,128)})) %all-reduce.11.cloned.1.call-update) | async-done | bytes 67600 | tf_op jit(solution)/shard_map/psum | solution.py:141
  801.8 5.6 all-reduce.1
  809.1 104.3 %all-reduce.13.cloned.1.call-done = (f32[4,512,256]{1,2,0:T(8,128)}, f32[4,64,256]{2,1,0:T(8,128)}) async-done(((f32[4,512,256]{1,2,0:T(8,128)}, f32[4,64,256]{2,1,0:T(8,128)}), (f32[4,512,256]{1,2,0:T(8,128)}, f32[4,64,256]{2,1,0:T(8,128)})) %all-reduce.13.cloned.1.call-update) | async-done | bytes 2359312 | tf_op jit(solution)/shard_map/psum | solution.py:141
  913.3 2.9 copy.41
  916.2 1.7 pad_maximum_fusion.2
  917.9 1.5 copy.62
  919.5 1.3 copy.63
  (74 shorter events, 8.9 us)
Async XLA Ops:
  7.2 123.8 %copy-start = (bf16[512,256]{1,0:T(8,128)(2,1)S(1)}, bf16[512,256]{1,0:T(8,128)(2,1)}, u32[]{:S(2)}) copy-start(bf16[512,256]{1,0:T(8,128)(2,1)} %param.10) | copy-start | bytes 786436
  7.2 12.8 %copy-start.2 = (bf16[24,128,512]{2,1,0:T(8,128)(2,1)S(1)}, bf16[24,128,512]{2,1,0:T(8,128)(2,1)}, u32[]{:S(2)}) copy-start(bf16[24,128,512]{2,1,0:T(8,128)(2,1)} %param.7) | copy-start | bytes 9437188
  7.2 125.0 %copy-start.13 = (f32[3,3,3,512]{3,2,1,0:T(4,128)S(1)}, f32[3,3,3,512]{3,2,1,0:T(4,128)}, u32[]{:S(2)}) copy-start(f32[3,3,3,512]{3,2,1,0:T(4,128)} %param.8) | copy-start | bytes 165892
  7.2 236.6 %reduce-scatter.4.cloned.1.call-start = ((), (), s32[]{:S(2)}) async-start(), calls=%async_computation.2 | async-start | bytes 163840
  12.4 121.8 %collective-permute-start = (bf16[18,128,512]{2,1,0:T(8,128)(2,1)}, bf16[18,128,512]{2,1,0:T(8,128)(2,1)}, u32[]{:S(2)}, u32[]{:S(2)}) collective-permute-start(bf16[18,128,512]{2,1,0:T(8,128)(2,1)} %get-tuple-element.56), channel_id=1, source_target_pairs={{0,4},{4,8},{8,12},{12,16},{16,20},{20,24},{24,28},{1,5},{5,9},{9,... | collective-permute-start | bytes 7077896 | tf_op jit(solution)/shard_map/ppermute | solution.py:24
  18.7 115.5 %collective-permute-start.1 = (bf16[18,128,512]{2,1,0:T(8,128)(2,1)}, bf16[18,128,512]{2,1,0:T(8,128)(2,1)}, u32[]{:S(2)}, u32[]{:S(2)}) collective-permute-start(bf16[18,128,512]{2,1,0:T(8,128)(2,1)} %get-tuple-element.57), channel_id=1, source_target_pairs={{4,0},{8,4},{12,8},{16,12},{20,16},{24,20},{28,24},{5,1},{9,5},{13... | collective-permute-start | bytes 7077896 | tf_op jit(solution)/shard_map/ppermute | solution.py:27
  132.1 329.7 %all-reduce.9.cloned.1.call-start = ((), (), s32[]{:S(2)}) async-start(), calls=%async_computation.3 | async-start | bytes 25165824
  166.3 2.1 copy-start.4
  187.7 1.7 copy-start.3
  217.6 1.6 copy-start.5
  217.6 4.0 copy-start.6
  241.8 0.7 copy-start.17
  241.8 2.8 copy-start.15
  241.9 354.5 %all-gather.3.cloned.1.call-start = ((), (), s32[]{:S(2)}) async-start(), calls=%async_computation.1 | async-start | bytes 7864320 | tf_op jit(solution)/shard_map/all_gather | solution.py:121
  464.0 81.0 %copy-start.8 = (f32[4,3072,64]{1,0,2:T(4,128)}, f32[4,3072,64]{1,0,2:T(4,128)S(1)}, u32[]{:S(2)}) copy-start(f32[4,3072,64]{1,0,2:T(4,128)S(1)} %constant_dynamic-slice_fusion) | copy-start | bytes 9437188
  466.1 6.8 copy-start.12
  466.1 5.7 collective-permute-start.2
  472.3 70.7 %copy-start.14 = (bf16[256,11]{0,1:T(8,128)(2,1)S(1)}, bf16[256,11]{0,1:T(8,128)(2,1)}, u32[]{:S(2)}) copy-start(bf16[256,11]{0,1:T(8,128)(2,1)} %param.12) | copy-start | bytes 16900
  472.3 70.2 %collective-permute-start.3 = (f32[3072,256]{1,0:T(8,128)S(1)}, f32[3072,256]{1,0:T(8,128)S(1)}, u32[]{:S(2)}, u32[]{:S(2)}) collective-permute-start(f32[3072,256]{1,0:T(8,128)S(1)} %add.130), channel_id=1, source_target_pairs={{0,2},{1,3},{2,0},{3,1},{4,6},{5,7},{6,4},{7,5},{8,10},{9,11},{10,... | collective-permute-start | bytes 9437192 | tf_op jit(solution)/shard_map/ppermute | solution.py:15
  543.0 4.3 copy-start.7
  543.0 1.9 copy-start.16
  544.9 2.3 copy-start.9
  549.7 251.0 %all-reduce.11.cloned.1.call-start = ((), (), s32[]{:S(2)}) async-start(), calls=%async_computation.4 | async-start | bytes 182272 | tf_op jit(solution)/shard_map/psum | solution.py:141
  622.5 4.3 copy-start.10
  658.9 4.3 copy-start.11
  726.5 194.3 %copy-start.1 = (bf16[512,256]{1,0:T(8,128)(2,1)S(1)}, bf16[512,256]{1,0:T(8,128)(2,1)}, u32[]{:S(2)}) copy-start(bf16[512,256]{1,0:T(8,128)(2,1)} %param.10) | copy-start | bytes 786436
  730.4 183.0 %all-reduce.13.cloned.1.call-start = ((), (), s32[]{:S(2)}) async-start(), calls=%async_computation.5 | async-start | bytes 4718592 | tf_op jit(solution)/shard_map/psum | solution.py:141
Sparse Core Ops, SparseCore 0:
  132.2 18.7 reduce-scatter.3
  242.0 219.8 all-reduce.8
  549.8 46.5 all-gather.2
  730.5 70.0 all-reduce.10
  805.1 108.2 all-reduce.12
